TPU v7x, 32 devices: a whole 2x2x4 slice. The times are simulated.
32 devices in a mesh: gz: 8 (over z, y), gy: 4 (over x, core).
Axes of the slice: x: 2, y: 2, z: 4, core: 2. Of those that a mesh axis runs over, the one named last changes fastest.
Arguments:
- state: bfloat16 [5, 8, 768, 1536], P(None, None, 'gy', 'gz'), may hold values from -6 to 6
- visc_base: bfloat16 [8, 768, 1536], P(None, 'gy', 'gz'), may hold values from 0.29882812 to 3
- dz_op: bfloat16 [1536, 1536], replicated, may hold values from -0.15625 to 0.15625
- dy_op: bfloat16 [768, 768], replicated, may hold values from -0.21875 to 0.21875
Outputs:
- new_state: bfloat16 [5, 8, 768, 1536], P(None, None, 'gy', 'gz')
All inputs are finite; a program needn't handle non-finite values.
Results may differ from a plain program's by a relative error of at most 0.011.
Values may be sent and summed in bfloat16 or wider, within the bound.
A program may use at most 128 MiB of HBM per device.

v0:
```python
from functools import partial

import jax
import jax.numpy as jnp
from jax import lax
from jax.sharding import PartitionSpec as P


def apply_line(items, operator):
    shape_in = items.shape
    result = jnp.dot(
        items.reshape(-1, operator.shape[0]), operator, preferred_element_type=jnp.float32
    )
    return result.astype(jnp.bfloat16).reshape(shape_in)


def keep_items(items):
    return items


def into_zlines(values, handler):
    layers, planes, ylocal, zlocal = values.shape
    flattened = values.reshape(layers, planes * ylocal, zlocal)
    return handler(lax.all_to_all(flattened, "gz", split_axis=1, concat_axis=2, tiled=True))


def from_zlines(values, planes, ylocal):
    returned = lax.all_to_all(values, "gz", split_axis=2, concat_axis=1, tiled=True)
    return returned.reshape(returned.shape[0], planes, ylocal, returned.shape[2])


def into_ylines(values, handler):
    layers, planes, ylocal, zlocal = values.shape
    turned = jnp.swapaxes(values, 2, 3).reshape(layers, planes * zlocal, ylocal)
    return handler(lax.all_to_all(turned, "gy", split_axis=1, concat_axis=2, tiled=True))


def from_ylines(values, planes, zlocal):
    returned = lax.all_to_all(values, "gy", split_axis=2, concat_axis=1, tiled=True)
    layers = returned.shape[0]
    return jnp.swapaxes(returned.reshape(layers, planes, zlocal, returned.shape[2]), 2, 3)


def viscosity(dens_y, dens_z, visc_base):
    sensor = dens_y.astype(jnp.float32) ** 2 + dens_z.astype(jnp.float32) ** 2
    return (visc_base.astype(jnp.float32) * (0.5 + sensor / (1.0 + sensor))).astype(jnp.bfloat16)


def product(visc, gradient):
    return (visc.astype(jnp.float32) * gradient.astype(jnp.float32)).astype(jnp.bfloat16)


def on_device(state, visc_base, dz_op, dy_op):
    planes, ylocal, zlocal = visc_base.shape
    zderive = partial(apply_line, operator=dz_op)
    yderive = partial(apply_line, operator=dy_op)
    zline_grad = into_zlines(state, zderive)
    yline_grad = into_ylines(state, yderive)
    dens_z = from_zlines(zline_grad[0:1], planes, ylocal)
    dens_y = from_ylines(yline_grad[0:1], planes, zlocal)
    visc = viscosity(dens_y[0], dens_z[0], visc_base)
    visc_z = into_zlines(visc[None], keep_items)
    visc_y = into_ylines(visc[None], keep_items)
    div_z = from_zlines(apply_line(product(visc_z, zline_grad), dz_op), planes, ylocal)
    div_y = from_ylines(apply_line(product(visc_y, yline_grad), dy_op), planes, zlocal)
    total = state.astype(jnp.float32) + 0.5 * (
        div_y.astype(jnp.float32) + div_z.astype(jnp.float32)
    )
    return total.astype(jnp.bfloat16)


def solution(mesh):
    return jax.shard_map(
        on_device,
        mesh=mesh,
        in_specs=(P(None, None, "gy", "gz"), P(None, "gy", "gz"), P(), P()),
        out_specs=P(None, None, "gy", "gz"),
        check_vma=False,
    )
```

profile of v0, /device:TPU:0, one launch (start us, length us, event | category | flops | bytes accessed | tf_op | source)
XLA Modules:
  0.0 436.5 jit_solution(13276210200379268121)
XLA Ops:
  0.0 9.3 %copy.101 = bf16[5,8,192,192]{3,0,2,1:T(8,128)(2,1)} copy(bf16[5,8,192,192]{2,3,1,0:T(8,128)(2,1)} %bitcast.100) | data formatting | bytes 5898240 | tf_op jit(solution)/shard_map/reshape | solution.py:34
  9.3 8.1 %reshape.98 = bf16[4,2,184320]{2,1,0:T(2,128)(2,1)} reshape(bf16[1536,5,192]{2,1,0:T(8,128)(2,1)} %bitcast.105) | data formatting | bytes 5898240
  17.4 4.6 %all-to-all-start = ((bf16[4,2,184320]{2,1,0:T(2,128)(2,1)}), bf16[4,2,184320]{2,1,0:T(2,128)(2,1)}, u32[]{:S(2)}, u32[]{:S(2)}) async-start(bf16[4,2,184320]{2,1,0:T(2,128)(2,1)} %reshape.98), calls=%async_computation | async-start | bytes 5898240 | tf_op jit(solution)/shard_map/all_to_all | solution.py:35
  22.0 7.6 %copy.82 = bf16[5,8,192,192]{3,0,2,1:T(8,128)(2,1)} copy(bf16[5,8,192,192]{3,2,1,0:T(8,128)(2,1)} %param.4) | data formatting | bytes 5898240 | tf_op args[0]
  29.6 9.3 %reshape.94 = bf16[8,2,92160]{2,1,0:T(2,128)(2,1)} reshape(bf16[1536,5,192]{2,1,0:T(8,128)(2,1)} %bitcast.106) | data formatting | bytes 5898240
  38.9 18.7 %all-to-all-done = bf16[4,2,184320]{2,1,0:T(2,128)(2,1)} async-done(((bf16[4,2,184320]{2,1,0:T(2,128)(2,1)}), bf16[4,2,184320]{2,1,0:T(2,128)(2,1)}, u32[]{:S(2)}, u32[]{:S(2)}) %all-to-all-start) | async-done | bytes 2949152 | tf_op jit(solution)/shard_map/all_to_all | solution.py:35
  57.6 6.9 %all-to-all-start.2 = ((bf16[8,2,92160]{2,1,0:T(2,128)(2,1)}), bf16[8,2,92160]{2,1,0:T(2,128)(2,1)}, u32[]{:S(2)}, u32[]{:S(2)}) async-start(bf16[8,2,92160]{2,1,0:T(2,128)(2,1)} %reshape.94), calls=%async_computation.2 | async-start | bytes 5898240 | tf_op jit(solution)/shard_map/all_to_all | solution.py:24
  64.5 8.2 %reshape.99 = bf16[1536,5,192]{2,1,0:T(8,128)(2,1)} reshape(bf16[4,2,184320]{2,1,0:T(2,128)(2,1)} %all-to-all-done) | data formatting | bytes 5898240
  72.6 8.1 %copy.111 = bf16[5,4,384,192]{3,1,2,0:T(4,128)(2,1)} copy(bf16[5,4,384,192]{3,0,2,1:T(8,128)(2,1)} %bitcast.101) | data formatting | bytes 5898240 | tf_op jit(solution)/shard_map/all_to_all | solution.py:35
  80.8 7.8 %reshape.78 = bf16[1920,768]{1,0:T(8,128)(2,1)} reshape(bf16[5,384,4,192]{3,2,1,0:T(4,128)(2,1)} %bitcast.107) | data formatting | bytes 5898240 | tf_op jit(solution)/shard_map/reshape | solution.py:12
  88.6 4.3 convolution_convert_fusion.3
  92.9 1.6 copy-done.3
  94.6 1.3 copy.79
  96.4 4.2 reduce.1
  101.6 29.2 %all-to-all-done.2 = bf16[8,2,92160]{2,1,0:T(2,128)(2,1)} async-done(((bf16[8,2,92160]{2,1,0:T(2,128)(2,1)}), bf16[8,2,92160]{2,1,0:T(2,128)(2,1)}, u32[]{:S(2)}, u32[]{:S(2)}) %all-to-all-start.2) | async-done | bytes 2949152 | tf_op jit(solution)/shard_map/all_to_all | solution.py:24
  130.8 4.6 %all-to-all-start.1 = ((bf16[4,2,36864]{2,1,0:T(2,128)(2,1)}), bf16[4,2,36864]{2,1,0:T(2,128)(2,1)}, u32[]{:S(2)}, u32[]{:S(2)}) async-start(bf16[4,2,36864]{2,1,0:T(2,128)(2,1)} %reshape.100), calls=%async_computation.1 | async-start | bytes 1179648 | tf_op jit(solution)/shard_map/all_to_all | solution.py:39
  135.4 9.3 %reshape.95 = bf16[1536,5,192]{2,1,0:T(8,128)(2,1)} reshape(bf16[8,2,92160]{2,1,0:T(2,128)(2,1)} %all-to-all-done.2) | data formatting | bytes 5898240
  144.7 7.3 %copy.84 = bf16[5,192,8,192]{3,2,1,0:T(8,128)(2,1)} copy(bf16[5,192,8,192]{3,0,1,2:T(8,128)(2,1)} %bitcast.102) | data formatting | bytes 5898240 | tf_op jit(solution)/shard_map/all_to_all | solution.py:24
  152.0 7.2 %reshape.80 = bf16[960,1536]{1,0:T(8,128)(2,1)} reshape(bf16[5,192,8,192]{3,2,1,0:T(8,128)(2,1)} %copy.84) | data formatting | bytes 5898240 | tf_op jit(solution)/shard_map/reshape | solution.py:12
  159.2 8.0 %convolution_convert_fusion.1 = bf16[960,1536]{1,0:T(8,128)(2,1)S(1)} fusion(bf16[960,1536]{1,0:T(8,128)(2,1)} %reshape.80, bf16[1536,1536]{1,0:T(8,128)(2,1)} %param.6), kind=kOutput, calls=%fused_computation.11 | convolution fusion | flops 4531322880 | bytes 10616832 | tf_op jit(solution)/shard_map/dot_general | solution.py:11
  167.2 1.6 copy-done.4
  168.8 1.2 copy.85
  170.1 8.9 %reduce = bf16[1536,192]{1,0:T(8,128)(2,1)S(1)} reduce(bf16[1536,1,192]{2,1,0:T(2,128)(2,1)S(1)} %bitcast.111, bf16[]{:T(256)} %broadcast.2), dimensions={1}, to_apply=%bitcast.79.reduce_sub_computation | reduce | bytes 1179650
  178.9 1.8 reshape.96
  180.7 3.8 all-to-all-start.3
  184.6 2.3 reshape.101
  187.7 1.7 integer_pow.21
  189.4 11.7 %all-to-all-done.3 = bf16[8,2,18432]{2,1,0:T(2,128)(2,1)S(1)} async-done(((bf16[8,2,18432]{2,1,0:T(2,128)(2,1)}), bf16[8,2,18432]{2,1,0:T(2,128)(2,1)S(1)}, u32[]{:S(2)}, u32[]{:S(2)}) %all-to-all-start.3) | async-done | bytes 589856 | tf_op jit(solution)/shard_map/all_to_all | solution.py:28
  201.2 1.2 reshape.97
  202.4 2.6 copy.86
  205.0 2.4 convert_multiply_fusion.1
  207.3 2.7 integer_pow.24
  210.1 2.2 fusion.7
  212.3 1.5 reshape.81
  213.8 3.5 copy.87
  217.3 9.8 %reduce.3 = bf16[1536,192]{1,0:T(8,128)(2,1)} reduce(bf16[1536,1,192]{2,1,0:T(2,128)(2,1)S(1)} %bitcast.112, bf16[]{:T(256)} %broadcast.2), dimensions={1}, to_apply=%bitcast.89.reduce_sub_computation | reduce | bytes 1179650
  227.0 3.1 reshape.106
  230.1 4.1 all-to-all-start.4
  234.8 8.9 %reduce.2 = bf16[1536,192]{1,0:T(8,128)(2,1)S(1)} reduce(bf16[1536,1,192]{2,1,0:T(2,128)(2,1)S(1)} %bitcast.110, bf16[]{:T(256)} %broadcast.2), dimensions={1}, to_apply=%bitcast.85.reduce_sub_computation | reduce | bytes 1179650
  243.6 1.7 reshape.102
  245.3 4.4 %all-to-all-start.6 = ((bf16[8,2,18432]{2,1,0:T(2,128)(2,1)}), bf16[8,2,18432]{2,1,0:T(2,128)(2,1)}, u32[]{:S(2)}, u32[]{:S(2)}) async-start(bf16[8,2,18432]{2,1,0:T(2,128)(2,1)} %reshape.102), calls=%async_computation.6 | async-start | bytes 1179648 | tf_op jit(solution)/shard_map/all_to_all | solution.py:24
  249.8 2.6 reshape.107
  254.2 2.5 fusion.4
  256.7 4.1 convolution_convert_fusion.2
  260.8 6.6 %copy.91 = bf16[5,384,768]{1,0,2:T(8,128)(2,1)} copy(bf16[5,384,768]{2,1,0:T(8,128)(2,1)} %bitcast.123) | data formatting | bytes 5898240 | tf_op jit(solution)/shard_map/reshape | solution.py:14
  267.5 4.9 %all-to-all-start.5 = ((bf16[5,384,768]{1,0,2:T(8,128)(2,1)}), bf16[5,384,768]{1,0,2:T(8,128)(2,1)}, u32[]{:S(2)}, u32[]{:S(2)}) async-start(bf16[5,384,768]{1,0,2:T(8,128)(2,1)} %copy.91), calls=%async_computation.5 | async-start | bytes 9437184 | tf_op jit(solution)/shard_map/all_to_all | solution.py:39
  272.4 4.3 reshape.103
  278.1 2.1 copy.97
  280.3 1.9 reshape.85
  282.2 2.5 fusion.3
  284.6 8.4 %convolution_convert_fusion = bf16[960,1536]{1,0:T(8,128)(2,1)} fusion(bf16[960,1536]{1,0:T(8,128)(2,1)S(1)} %fusion.3, bf16[1536,1536]{1,0:T(8,128)(2,1)} %param.6), kind=kOutput, calls=%fused_computation.10 | convolution fusion | flops 4531322880 | bytes 10616832 | tf_op jit(solution)/shard_map/dot_general | solution.py:11
  293.1 8.4 %copy.98 = bf16[5,192,1536]{1,0,2:T(8,128)(2,1)} copy(bf16[5,192,1536]{2,1,0:T(8,128)(2,1)} %bitcast.122) | data formatting | bytes 5898240 | tf_op jit(solution)/shard_map/reshape | solution.py:14
  301.5 9.3 %reshape.104 = bf16[8,2,92160]{2,1,0:T(2,128)(2,1)} reshape(bf16[1536,5,192]{2,1,0:T(8,128)(2,1)} %bitcast.103) | data formatting | bytes 5898240
  310.8 15.4 %all-to-all-done.5 = bf16[5,384,768]{1,0,2:T(8,128)(2,1)} async-done(((bf16[5,384,768]{1,0,2:T(8,128)(2,1)}), bf16[5,384,768]{1,0,2:T(8,128)(2,1)}, u32[]{:S(2)}, u32[]{:S(2)}) %all-to-all-start.5) | async-done | bytes 2949152 | tf_op jit(solution)/shard_map/all_to_all | solution.py:39
  326.2 6.3 %all-to-all-start.7 = ((bf16[8,2,92160]{2,1,0:T(2,128)(2,1)}), bf16[8,2,92160]{2,1,0:T(2,128)(2,1)}, u32[]{:S(2)}, u32[]{:S(2)}) async-start(bf16[8,2,92160]{2,1,0:T(2,128)(2,1)} %reshape.104), calls=%async_computation.7 | async-start | bytes 5898240 | tf_op jit(solution)/shard_map/all_to_all | solution.py:28
  332.5 2.7 copy.92
  335.9 6.4 %copy.93 = f32[5,4,384,192]{2,1,3,0:T(4,128)} copy(f32[5,4,384,192]{2,3,1,0:T(8,128)S(1)} %convert_bitcast_fusion) | data formatting | bytes 11796480 | tf_op jit(solution)/shard_map/convert_element_type | solution.py:67
  342.3 8.8 %reshape.87 = f32[5,8,192,192]{2,1,3,0:T(8,128)} reshape(f32[5,4,384,192]{2,1,3,0:T(4,128)} %copy.93) | data formatting | bytes 11796480 | tf_op jit(solution)/shard_map/convert_element_type | solution.py:67
  351.1 47.8 %all-to-all-done.7 = bf16[8,2,92160]{2,1,0:T(2,128)(2,1)} async-done(((bf16[8,2,92160]{2,1,0:T(2,128)(2,1)}), bf16[8,2,92160]{2,1,0:T(2,128)(2,1)}, u32[]{:S(2)}, u32[]{:S(2)}) %all-to-all-start.7) | async-done | bytes 2949152 | tf_op jit(solution)/shard_map/all_to_all | solution.py:28
  398.9 9.3 %reshape.105 = bf16[1536,5,192]{2,1,0:T(8,128)(2,1)} reshape(bf16[8,2,92160]{2,1,0:T(2,128)(2,1)} %all-to-all-done.7) | data formatting | bytes 5898240
  408.2 7.2 %copy.99 = bf16[5,192,1536]{2,1,0:T(8,128)(2,1)} copy(bf16[5,192,1536]{1,0,2:T(8,128)(2,1)} %bitcast.104) | data formatting | bytes 5898240 | tf_op jit(solution)/shard_map/all_to_all | solution.py:28
  415.3 7.2 %reshape.88 = f32[5,192,8,192]{3,2,1,0:T(8,128)} reshape(bf16[5,192,1536]{2,1,0:T(8,128)(2,1)} %copy.99) | data formatting | bytes 8847360 | tf_op jit(solution)/shard_map/convert_element_type | solution.py:67
  422.6 10.7 %fusion.2 = bf16[5,8,192,192]{3,1,2,0:T(8,128)(2,1)S(1)} fusion(f32[5,192,8,192]{3,2,1,0:T(8,128)} %reshape.88, f32[5,8,192,192]{2,1,3,0:T(8,128)} %reshape.87, bf16[5,8,192,192]{3,2,1,0:T(8,128)(2,1)} %param.4), kind=kLoop, calls=%fused_computation.3 | loop fusion | flops 7372800 | bytes 17694720 | tf_op jit(solution)/shard_map/convert_element_type | solution.py:69
  433.2 2.9 copy.100
  (26 shorter events, 6.8 us)
Async XLA Ops:
  0.0 88.6 %copy-start = (bf16[768,768]{1,0:T(8,128)(2,1)S(1)}, bf16[768,768]{1,0:T(8,128)(2,1)}, u32[]{:S(2)}) copy-start(bf16[768,768]{1,0:T(8,128)(2,1)} %param.7) | copy-start | bytes 3538948
  17.4 40.2 %all-to-all-start = ((bf16[4,2,184320]{2,1,0:T(2,128)(2,1)}), bf16[4,2,184320]{2,1,0:T(2,128)(2,1)}, u32[]{:S(2)}, u32[]{:S(2)}) async-start(bf16[4,2,184320]{2,1,0:T(2,128)(2,1)} %reshape.98), calls=%async_computation | async-start | bytes 5898240 | tf_op jit(solution)/shard_map/all_to_all | solution.py:35
  57.6 73.2 %all-to-all-start.2 = ((bf16[8,2,92160]{2,1,0:T(2,128)(2,1)}), bf16[8,2,92160]{2,1,0:T(2,128)(2,1)}, u32[]{:S(2)}, u32[]{:S(2)}) async-start(bf16[8,2,92160]{2,1,0:T(2,128)(2,1)} %reshape.94), calls=%async_computation.2 | async-start | bytes 5898240 | tf_op jit(solution)/shard_map/all_to_all | solution.py:24
  92.9 1.6 copy-start.3
  130.8 49.9 %all-to-all-start.1 = ((bf16[4,2,36864]{2,1,0:T(2,128)(2,1)}), bf16[4,2,36864]{2,1,0:T(2,128)(2,1)}, u32[]{:S(2)}, u32[]{:S(2)}) async-start(bf16[4,2,36864]{2,1,0:T(2,128)(2,1)} %reshape.100), calls=%async_computation.1 | async-start | bytes 1179648 | tf_op jit(solution)/shard_map/all_to_all | solution.py:39
  167.2 1.6 copy-start.4
  180.7 20.5 %all-to-all-start.3 = ((bf16[8,2,18432]{2,1,0:T(2,128)(2,1)}), bf16[8,2,18432]{2,1,0:T(2,128)(2,1)S(1)}, u32[]{:S(2)}, u32[]{:S(2)}) async-start(bf16[8,2,18432]{2,1,0:T(2,128)(2,1)} %reshape.96), calls=%async_computation.3 | async-start | bytes 1179648 | tf_op jit(solution)/shard_map/all_to_all | solution.py:28
  205.0 5.1 %copy-start.2 = (f32[1,8,192,192]{2,1,3,0:T(8,128)S(1)}, f32[1,8,192,192]{2,1,3,0:T(8,128)}, u32[]{:S(2)}) copy-start(f32[1,8,192,192]{2,1,3,0:T(8,128)} %integer_pow.21) | copy-start | bytes 3538948
  230.1 15.3 %all-to-all-start.4 = ((bf16[4,2,36864]{2,1,0:T(2,128)(2,1)}), bf16[4,2,36864]{2,1,0:T(2,128)(2,1)}, u32[]{:S(2)}, u32[]{:S(2)}) async-start(bf16[4,2,36864]{2,1,0:T(2,128)(2,1)} %reshape.106), calls=%async_computation.4 | async-start | bytes 1179648 | tf_op jit(solution)/shard_map/all_to_all | solution.py:35
  245.3 22.1 %all-to-all-start.6 = ((bf16[8,2,18432]{2,1,0:T(2,128)(2,1)}), bf16[8,2,18432]{2,1,0:T(2,128)(2,1)}, u32[]{:S(2)}, u32[]{:S(2)}) async-start(bf16[8,2,18432]{2,1,0:T(2,128)(2,1)} %reshape.102), calls=%async_computation.6 | async-start | bytes 1179648 | tf_op jit(solution)/shard_map/all_to_all | solution.py:24
  267.5 58.8 %all-to-all-start.5 = ((bf16[5,384,768]{1,0,2:T(8,128)(2,1)}), bf16[5,384,768]{1,0,2:T(8,128)(2,1)}, u32[]{:S(2)}, u32[]{:S(2)}) async-start(bf16[5,384,768]{1,0,2:T(8,128)(2,1)} %copy.91), calls=%async_computation.5 | async-start | bytes 9437184 | tf_op jit(solution)/shard_map/all_to_all | solution.py:39
  326.2 72.6 %all-to-all-start.7 = ((bf16[8,2,92160]{2,1,0:T(2,128)(2,1)}), bf16[8,2,92160]{2,1,0:T(2,128)(2,1)}, u32[]{:S(2)}, u32[]{:S(2)}) async-start(bf16[8,2,92160]{2,1,0:T(2,128)(2,1)} %reshape.104), calls=%async_computation.7 | async-start | bytes 5898240 | tf_op jit(solution)/shard_map/all_to_all | solution.py:28
  422.6 13.5 %copy-start.1 = (bf16[768,768]{1,0:T(8,128)(2,1)S(1)}, bf16[768,768]{1,0:T(8,128)(2,1)}, u32[]{:S(2)}) copy-start(bf16[768,768]{1,0:T(8,128)(2,1)} %param.7) | copy-start | bytes 3538948
where the time goes:
time: 445 us; the launch traced here: 437 us
  local copies, waits for them, and re-layouts  196 us (44%)
  waiting for transfers between devices  123 us (28%)
  other arithmetic  52.7 us (12%)
  starting transfers between devices  39.7 us (9%)
  matrix products  24.8 us (6%)
    unnamed x26, local copies, waits for them, and re-layouts  82.7 us
    all_to_all x2, waiting for transfers between devices, from_zlines(): lax.all_to_all(values, 'gz', split_axis=2, concat_axis=1, tiled=True)  59.5 us
    unnamed x4, other arithmetic  31.7 us
    all_to_all x2, waiting for transfers between devices, into_zlines(): lax.all_to_all(flattened, 'gz', split_axis=1, concat_axis=2, tiled=True)  29.2 us
    dot_general x4, matrix products, apply_line(): jnp.dot(items.reshape(-1, operator.shape[0]), operator, preferred_element...  24.8 us
    all_to_all x2, waiting for transfers between devices, into_ylines(): lax.all_to_all(turned, 'gy', split_axis=1, concat_axis=2, tiled=True)  18.7 us
    all_to_all x2, waiting for transfers between devices, from_ylines(): lax.all_to_all(values, 'gy', split_axis=2, concat_axis=1, tiled=True)  15.4 us
    convert_element_type x2, local copies, waits for them, and re-layouts, on_device(): div_y.astype(jnp.float32) + div_z.astype(jnp.float32)  15.2 us
  transfers between devices with their start and end apart: 8, of which 5 were waited for; matrix products, arithmetic and copies ran while one was open for 43% of the time, Pallas kernels for 0%

commit v1 on v0

v1 whole, which is shorter than its diff:
```python
import functools

import jax
import jax.numpy as jnp
from jax import lax
from jax.experimental import pallas as pl
from jax.experimental.pallas import tpu as pltpu
from jax.sharding import PartitionSpec as P

F32 = jnp.float32
BF16 = jnp.bfloat16
MESH = pl.DeviceIdType.MESH
LANES = 128


def apply_line(items, operator):
    shape_in = items.shape
    result = jnp.dot(
        items.reshape(-1, operator.shape[0]), operator, preferred_element_type=F32
    )
    return result.astype(BF16).reshape(shape_in)


def into_zlines(values):
    layers, planes, ylocal, zlocal = values.shape
    flattened = values.reshape(layers, planes * ylocal, zlocal)
    return lax.all_to_all(flattened, "gz", split_axis=1, concat_axis=2, tiled=True)


def from_zlines(values, planes, ylocal):
    returned = lax.all_to_all(values, "gz", split_axis=2, concat_axis=1, tiled=True)
    return returned.reshape(returned.shape[0], planes, ylocal, returned.shape[2])


def into_ylines(values):
    layers, planes, ylocal, zlocal = values.shape
    turned = jnp.swapaxes(values, 2, 3).reshape(layers, planes * zlocal, ylocal)
    return lax.all_to_all(turned, "gy", split_axis=1, concat_axis=2, tiled=True)


def from_ylines(values, planes, zlocal):
    returned = lax.all_to_all(values, "gy", split_axis=2, concat_axis=1, tiled=True)
    layers = returned.shape[0]
    return jnp.swapaxes(returned.reshape(layers, planes, zlocal, returned.shape[2]), 2, 3)


def viscosity(dens_y, dens_z, visc_base):
    sensor = dens_y.astype(F32) ** 2 + dens_z.astype(F32) ** 2
    return (visc_base.astype(F32) * (0.5 + sensor / (1.0 + sensor))).astype(BF16)


def product(visc, gradient):
    return (visc.astype(F32) * gradient.astype(F32)).astype(BF16)


def by_lines(state, visc_base, dz_op, dy_op):
    planes, ylocal, zlocal = visc_base.shape
    zline_grad = apply_line(into_zlines(state), dz_op)
    yline_grad = apply_line(into_ylines(state), dy_op)
    dens_z = from_zlines(zline_grad[0:1], planes, ylocal)
    dens_y = from_ylines(yline_grad[0:1], planes, zlocal)
    visc = viscosity(dens_y[0], dens_z[0], visc_base)
    visc_z = into_zlines(visc[None])
    visc_y = into_ylines(visc[None])
    div_z = from_zlines(apply_line(product(visc_z, zline_grad), dz_op), planes, ylocal)
    div_y = from_ylines(apply_line(product(visc_y, yline_grad), dy_op), planes, zlocal)
    total = state.astype(F32) + 0.5 * (div_y.astype(F32) + div_z.astype(F32))
    return total.astype(BF16)


def pack(block, odd):
    rows, width = block.shape[-2:]
    half, whole = rows // 2, width - LANES // 2
    cat = jnp.concatenate
    e_rest = block[..., whole:]
    even = cat([block[..., :whole], cat([e_rest[..., :half, :], e_rest[..., half:, :]], -1)], -2)
    o_rest = block[..., : LANES // 2]
    odd_ = cat(
        [block[..., LANES // 2 :], cat([o_rest[..., half:, :], o_rest[..., :half, :]], -1)], -2
    )
    return jnp.where(odd, odd_, even)


def unpack(packed, rows, odd):
    cat = jnp.concatenate
    mid = LANES // 2
    body, rest = packed[..., :rows, :], packed[..., rows:, :]
    left, right = rest[..., :mid], rest[..., mid:]
    even = cat([body, cat([left, right], -2)], -1)
    odd_ = cat([cat([right, left], -2), body], -1)
    return jnp.where(odd, odd_, even)


def kernel(
    nz, ny, fields,
    sp, dz_h, dyt_h, out,
    rin, zst, yst, gz, gy, dz, dyt, g0, visc, vy, fz, fy, dvs, dvr, osend,
    in_s, in_r, fw_s, fw_r, dv_s, dv_r, g_s, g_r, v_s, v_r, out_s, out_r, w_sem,
):
    me_z, me_y = lax.axis_index("gz"), lax.axis_index("gy")
    yl, zfull = zst.shape[1], zst.shape[2]
    zw = yst.shape[2]
    pairs = nz // 2
    pw = zfull // pairs
    half = yl // 2
    slots = fields + 1

    def loop(lo, hi, body):
        def step(k, carry):
            body(k)
            return carry

        lax.fori_loop(lo, hi, step, 0)

    def remote(src, dst, ssem, rsem, axis, peer):
        return pltpu.make_async_remote_copy(
            src_ref=src, dst_ref=dst, send_sem=ssem, recv_sem=rsem,
            device_id={axis: peer}, device_id_type=MESH,
        )

    barrier = pltpu.get_barrier_semaphore()

    def greet(axis, me, n):
        def body(d):
            pl.semaphore_signal(
                barrier, inc=1, device_id={axis: lax.rem(me + d, n)}, device_id_type=MESH
            )

        loop(1, n, body)

    w1 = pltpu.make_async_copy(dz_h, dz, w_sem.at[0])
    w2 = pltpu.make_async_copy(dyt_h, dyt, w_sem.at[1])
    greet("gz", me_z, nz)
    greet("gy", me_y, ny)
    pl.semaphore_wait(barrier, nz + ny - 2)

    def own_in(s):
        return pltpu.make_async_copy(sp.at[s, me_z], rin.at[s, me_z], in_r.at[s, me_z])

    def in_copy(s, other, slot):
        return remote(
            sp.at[s, other], rin.at[s, slot], in_s.at[s, other], in_r.at[s, slot], "gz", other
        )

    def start_in(s):
        loop(1, nz, lambda d: in_copy(s, lax.rem(me_z + d, nz), me_z).start())
        own_in(s).start()

    def wait_in(s):
        loop(1, nz, lambda d: in_copy(s, lax.rem(me_z + d, nz), lax.rem(me_z + d, nz)).wait_recv())
        own_in(s).wait()

    def zcols(j):
        return pl.ds(pl.multiple_of(j * zw, LANES), zw)

    def yrows(j):
        return pl.ds(pl.multiple_of(j * yl, 16), yl)

    class Swap:
        def __init__(self, src, dst, ssem, rsem, to_y):
            self.src, self.dst, self.ssem, self.rsem, self.to_y = src, dst, ssem, rsem, to_y

        def piece(self, j):
            return self.src.at[:, zcols(j)] if self.to_y else self.src.at[yrows(j), :]

        def place(self, j):
            return self.dst.at[yrows(j), :] if self.to_y else self.dst.at[:, zcols(j)]

        def local(self):
            return pltpu.make_async_copy(self.piece(me_y), self.place(me_y), self.rsem.at[me_y])

        def copy(self, other, slot):
            return remote(
                self.piece(other), self.place(slot), self.ssem.at[other], self.rsem.at[slot],
                "gy", other,
            )

        def start(self):
            loop(1, ny, lambda d: self.copy(lax.rem(me_y + d, ny), me_y).start())
            self.local().start()

        def wait(self):
            def body(d):
                other = lax.rem(me_y + d, ny)
                self.copy(other, other).wait_recv()

            loop(1, ny, body)
            self.local().wait()

        def sent(self):
            loop(1, ny, lambda d: self.copy(lax.rem(me_y + d, ny), me_y).wait_send())

    def forward(f, s):
        return Swap(zst.at[s], yst.at[f], fw_s.at[f], fw_r.at[f], True)

    def divs(f):
        return Swap(dvs.at[f], dvr.at[f], dv_s.at[f], dv_r.at[f], False)

    dens_y = Swap(gy.at[0], g0, g_s, g_r, False)
    visc_y = Swap(visc, vy, v_s, v_r, True)

    def out_copy(f, other, slot):
        return remote(
            osend.at[f, other], out.at[f, slot], out_s.at[f, other], out_r.at[f, slot],
            "gz", other,
        )

    def own_out(f):
        return pltpu.make_async_copy(osend.at[f, me_z], out.at[f, me_z], out_r.at[f, me_z])

    def pair_cols(m):
        return pl.multiple_of(m * pw, LANES)

    low = lax.broadcasted_iota(jnp.int32, (half, LANES), 1) < LANES // 2

    def turn(x):
        return pltpu.roll(x, LANES // 2, 1)

    def gather_lines(s):
        wait_in(s)

        def body(m):
            c = pair_cols(m)
            zst[s, :, pl.ds(c, pw // 3)] = rin[s, 2 * m, :yl, :]
            zst[s, :, pl.ds(pl.multiple_of(c + 2 * LANES, LANES), LANES)] = rin[
                s, 2 * m + 1, :yl, :
            ]
            pe = rin[s, 2 * m, yl:, :].astype(F32)
            po = rin[s, 2 * m + 1, yl:, :].astype(F32)
            mid = pl.ds(pl.multiple_of(c + LANES, LANES), LANES)
            zst[s, :half, mid] = jnp.where(low, pe, po).astype(BF16)
            zst[s, half:, mid] = turn(jnp.where(low, po, pe)).astype(BF16)

        loop(0, pairs, body)

    def grad_z(f, s):
        def body(m):
            cols = pl.ds(pair_cols(m), pw)
            gz[f, :, cols] = jnp.dot(
                zst[s], dz[:, cols], preferred_element_type=F32
            ).astype(BF16)

        loop(0, pairs, body)

    def grad_y(f):
        def body(r):
            rows = yrows(r)
            gy[f, rows, :] = jnp.dot(
                dyt[rows, :], yst[f], preferred_element_type=F32
            ).astype(BF16)

        loop(0, ny, body)

    def stage_a(f, s):
        gather_lines(s)
        forward(f, s).start()
        grad_z(f, s)

    def stage_b(f, s):
        forward(f, s).wait()
        grad_y(f)

    def viscosity_lines():
        def body(m):
            cols = pl.ds(pair_cols(m), pw)
            a, b = g0[:, cols].astype(F32), gz[0, :, cols].astype(F32)
            sensor = a * a + b * b
            visc[:, cols] = (
                zst[1, :, cols].astype(F32) * (0.5 + sensor / (1.0 + sensor))
            ).astype(BF16)

        loop(0, pairs, body)

    def stage_c(f):
        def weigh(r):
            rows = yrows(r)
            fy[rows, :] = (vy[rows, :].astype(F32) * gy[f, rows, :].astype(F32)).astype(BF16)

        loop(0, ny, weigh)

        def body(r):
            rows = yrows(r)
            dvs[f, rows, :] = jnp.dot(
                dyt[rows, :], fy[...], preferred_element_type=F32
            ).astype(BF16)

        loop(0, ny, body)
        divs(f).start()

    def stage_d(f, s):
        def weigh(m):
            cols = pl.ds(pair_cols(m), pw)
            fz[:, cols] = (visc[:, cols].astype(F32) * gz[f, :, cols].astype(F32)).astype(BF16)

        loop(0, pairs, weigh)
        divs(f).wait()

        def body(m):
            cols = pl.ds(pair_cols(m), pw)
            div = jnp.dot(fz[...], dz[:, cols], preferred_element_type=F32)
            div = div.astype(BF16).astype(F32)
            new = zst[s, :, cols].astype(F32) + 0.5 * (dvr[f, :, cols].astype(F32) + div)
            osend[f, 2 * m, :yl, :] = new[:, :LANES].astype(BF16)
            osend[f, 2 * m + 1, :yl, :] = new[:, 2 * LANES :].astype(BF16)
            top = new[:half, LANES : 2 * LANES]
            bottom = turn(new[half:, LANES : 2 * LANES])
            osend[f, 2 * m, yl:, :] = jnp.where(low, top, bottom).astype(BF16)
            osend[f, 2 * m + 1, yl:, :] = jnp.where(low, bottom, top).astype(BF16)

        loop(0, pairs, body)
        loop(1, nz, lambda d: out_copy(f, lax.rem(me_z + d, nz), me_z).start())
        own_out(f).start()

    loop(0, slots, start_in)
    w1.start()
    w2.start()
    w1.wait()
    w2.wait()
    stage_a(0, 0)
    stage_b(0, 0)
    dens_y.start()
    gather_lines(1)
    dens_y.wait()
    viscosity_lines()
    visc_y.start()
    stage_a(1, 2)
    stage_b(1, 2)
    visc_y.wait()

    def field(f):
        stage_c(f)

        @pl.when(f + 2 < fields)
        def _():
            stage_a(f + 2, f + 3)

        stage_d(f, jnp.where(f == 0, 0, f + 1))

        @pl.when(f + 2 < fields)
        def _():
            stage_b(f + 2, f + 3)

    loop(0, fields, field)

    def sent_in(s):
        loop(1, nz, lambda d: in_copy(s, lax.rem(me_z + d, nz), me_z).wait_send())

    loop(0, slots, sent_in)
    dens_y.sent()
    visc_y.sent()

    def finish(f):
        forward(f, jnp.where(f == 0, 0, f + 1)).sent()
        divs(f).sent()

        def body(d):
            other = lax.rem(me_z + d, nz)
            out_copy(f, other, other).wait_recv()
            out_copy(f, other, me_z).wait_send()

        loop(1, nz, body)
        own_out(f).wait()

    loop(0, fields, finish)


def by_planes(nz, ny, state, visc_base, dz_op, dy_op):
    fields, planes, yl, zl = state.shape
    zfull, yfull = dz_op.shape[0], dy_op.shape[0]
    zw = zfull // ny
    slots = fields + 1
    prow = yl + yl // 2
    odd = lax.rem(lax.axis_index("gz"), 2) == 1
    sp = pack(jnp.concatenate([state[:1], visc_base[None], state[1:]], 0), odd)
    any_ = pl.BlockSpec(memory_space=pl.ANY)
    vm = lambda *shape: pltpu.VMEM(shape, BF16)
    dma = lambda *shape: pltpu.SemaphoreType.DMA(shape)
    packed = pl.pallas_call(
        functools.partial(kernel, nz, ny, fields),
        out_shape=jax.ShapeDtypeStruct((fields, planes, prow, LANES), BF16),
        in_specs=[any_] * 3,
        out_specs=any_,
        scratch_shapes=[
            vm(slots, nz, prow, LANES),
            vm(slots, yl, zfull),
            vm(fields, yfull, zw),
            vm(fields, yl, zfull),
            vm(fields, yfull, zw),
            vm(zfull, zfull),
            vm(yfull, yfull),
            vm(yl, zfull),
            vm(yl, zfull),
            vm(yfull, zw),
            vm(yl, zfull),
            vm(yfull, zw),
            vm(fields, yfull, zw),
            vm(fields, yl, zfull),
            vm(fields, nz, prow, LANES),
            dma(slots, nz), dma(slots, nz),
            dma(fields, ny), dma(fields, ny),
            dma(fields, ny), dma(fields, ny),
            dma(ny), dma(ny), dma(ny), dma(ny),
            dma(fields, nz), dma(fields, nz),
            dma(2),
        ],
        compiler_params=pltpu.CompilerParams(
            collective_id=0, has_side_effects=True, vmem_limit_bytes=56 * 2**20
        ),
    )(sp, dz_op, dy_op.T)
    return unpack(packed, yl, odd)


def on_device(nz, ny, state, visc_base, dz_op, dy_op):
    planes, yl, zl = visc_base.shape
    if planes == nz and nz % 2 == 0 and zl == LANES + LANES // 2 and yl % 32 == 0:
        if dz_op.shape[0] % (LANES * ny) == 0:
            return by_planes(nz, ny, state, visc_base, dz_op, dy_op)
    return by_lines(state, visc_base, dz_op, dy_op)


def solution(mesh):
    return jax.shard_map(
        functools.partial(on_device, mesh.shape["gz"], mesh.shape["gy"]),
        mesh=mesh,
        in_specs=(P(None, None, "gy", "gz"), P(None, "gy", "gz"), P(), P()),
        out_specs=P(None, None, "gy", "gz"),
        check_vma=False,
    )
```

time: 445 us -> 177 us (0.40)
  the two profiles are of different devices: /device:TPU:0 before, /device:TPU:29 now
where the time goes in v1:
time: 177 us
  Pallas kernels  154 us (87%)
  local copies, waits for them, and re-layouts  12.4 us (7%)
  other arithmetic  10.4 us (6%)
    pallas_call x1, Pallas kernels, by_planes(): pl.pallas_call(functools.partial(kernel, nz, ny, fields), out_shape=jax.S...  154 us
    select_n x1, other arithmetic, pack(): return jnp.where(odd, odd_, even)  5.86 us
    unnamed x5, local copies, waits for them, and re-layouts  4.43 us
    select_n x1, other arithmetic, unpack(): return jnp.where(odd, odd_, even)  3.67 us

profile of v1, /device:TPU:29, one launch (start us, length us, event | category | flops | bytes accessed | tf_op | source)
XLA Modules:
  0.0 176.8 jit_solution(2260834163188360512)
XLA Ops:
  0.0 0.0 slice-start.1
  0.0 0.0 slice-start.2
  0.0 0.0 copy-start.1
  0.0 1.9 %slice-done.1 = bf16[4,8,192,192]{3,2,1,0:T(8,128)(2,1)S(1)} async-done(((bf16[5,8,192,192]{3,2,1,0:T(8,128)(2,1)}), bf16[4,8,192,192]{3,2,1,0:T(8,128)(2,1)S(1)}, s32[]{:S(2)}) %slice-start.1) | async-done | bytes 2359320 | tf_op jit(solution)/shard_map/slice | solution.py:374
  1.9 0.2 slice-done.2
  2.1 0.2 copy-done.1
  2.3 0.9 pad_maximum_fusion
  3.2 2.6 %fusion.1 = (bf16[6,8,96,64]{3,2,1,0:T(8,128)(2,1)S(1)}, bf16[6,8,96,64]{3,2,1,0:T(8,128)(2,1)}, bf16[6,8,96,64]{3,2,1,0:T(8,128)(2,1)}, bf16[6,8,96,64]{3,2,1,0:T(8,128)(2,1)}) fusion(bf16[6,8,192,192]{3,2,1,0:T(8,128)(2,1)S(1)} %pad_maximum_fusion), kind=kLoop, calls=%fused_computation.4 | loop fusion | bytes 4718592 | tf_op jit(solution)/shard_map/slice | solution.py:76
  5.8 2.7 %fusion = (bf16[6,8,192,128]{3,2,1,0:T(8,128)(2,1)S(1)}, bf16[6,8,192,128]{3,2,1,0:T(8,128)(2,1)}) fusion(bf16[6,8,192,192]{3,2,1,0:T(8,128)(2,1)S(1)} %pad_maximum_fusion), kind=kLoop, calls=%fused_computation.3 | loop fusion | bytes 9437184 | tf_op jit(solution)/shard_map/slice | solution.py:76
  8.5 5.9 %maximum_select_fusion.1.sp = bf16[6,8,288,128]{3,2,1,0:T(8,128)(2,1)} fusion(bf16[6,8,96,64]{3,2,1,0:T(8,128)(2,1)} %get-tuple-element.9, bf16[6,8,96,64]{3,2,1,0:T(8,128)(2,1)} %get-tuple-element.10, bf16[6,8,192,128]{3,2,1,0:T(8,128)(2,1)} %get-tuple-element.6, bf16[6,8,96,64]{3,2,1,0:T(8,128)(2,1)} %get-tuple-element.8, ...), kind=kLoop, calls=%fused_computation.2 | loop fusion | flops 23003136 | bytes 10616833 | tf_op jit(solution)/shard_map/jit(_where)/select_n | solution.py:81
  14.4 2.4 %copy.5 = bf16[768,768]{0,1:T(8,128)(2,1)} copy(bf16[768,768]{1,0:T(8,128)(2,1)} %param.7) | data formatting | bytes 2359296 | tf_op args[3]
  16.8 153.9 %shard_map.46 = bf16[5,8,288,128]{3,2,1,0:T(8,128)(2,1)} custom-call(bf16[6,8,288,128]{3,2,1,0:T(8,128)(2,1)} %maximum_select_fusion.1.sp, bf16[1536,1536]{1,0:T(8,128)(2,1)} %dz_h.1, bf16[768,768]{1,0:T(8,128)(2,1)} %bitcast.2), custom_call_target="tpu_custom_call" | custom-call | tf_op jit(solution)/shard_map/pallas_call | solution.py:378
  170.7 0.0 copy-start
  170.7 0.0 slice-start
  170.7 1.8 %copy-done = bf16[5,8,288,128]{3,2,1,0:T(8,128)(2,1)S(1)} copy-done((bf16[5,8,288,128]{3,2,1,0:T(8,128)(2,1)S(1)}, bf16[5,8,288,128]{3,2,1,0:T(8,128)(2,1)}, u32[]{:S(2)}) %copy-start) | copy-done | bytes 2949144
  172.5 0.4 fusion.2
  172.9 0.2 slice-done
  173.1 3.7 %maximum_select_fusion = bf16[5,8,192,192]{3,2,1,0:T(8,128)(2,1)} fusion(bf16[5,8,192,128]{3,2,1,0:T(8,128)(2,1)S(1)} %slice-done, bf16[5,8,96,64]{3,2,1,0:T(8,128)(2,1)S(1)} %get-tuple-element.12, bf16[5,8,96,64]{3,2,1,0:T(8,128)(2,1)S(1)} %get-tuple-element.11, pred[]{:T(512)S(6)} %eq.3), kind=kLoop, calls=%fused_computation.1 | loop fusion | flops 19169280 | bytes 5898241 | tf_op jit(solution)/shard_map/jit(_where)/select_n | solution.py:91
Async XLA Ops:
  0.0 1.9 %slice-start.1 = ((bf16[5,8,192,192]{3,2,1,0:T(8,128)(2,1)}), bf16[4,8,192,192]{3,2,1,0:T(8,128)(2,1)S(1)}, s32[]{:S(2)}) async-start(bf16[5,8,192,192]{3,2,1,0:T(8,128)(2,1)} %param.4), calls=%async_computation.1 | async-start | bytes 6291456 | tf_op jit(solution)/shard_map/slice | solution.py:374
  0.0 2.1 %slice-start.2 = ((bf16[5,8,192,192]{3,2,1,0:T(8,128)(2,1)}), bf16[1,8,192,192]{3,2,1,0:T(8,128)(2,1)S(1)}, s32[]{:S(2)}) async-start(bf16[5,8,192,192]{3,2,1,0:T(8,128)(2,1)} %param.4), calls=%async_computation.2 | async-start | bytes 1572864 | tf_op jit(solution)/shard_map/slice | solution.py:374
  0.0 2.3 %copy-start.1 = (bf16[8,192,192]{2,1,0:T(8,128)(2,1)S(1)}, bf16[8,192,192]{2,1,0:T(8,128)(2,1)}, u32[]{:S(2)}) copy-start(bf16[8,192,192]{2,1,0:T(8,128)(2,1)} %param.5) | copy-start | bytes 1769476
  170.7 1.8 %copy-start = (bf16[5,8,288,128]{3,2,1,0:T(8,128)(2,1)S(1)}, bf16[5,8,288,128]{3,2,1,0:T(8,128)(2,1)}, u32[]{:S(2)}) copy-start(bf16[5,8,288,128]{3,2,1,0:T(8,128)(2,1)} %shard_map.46) | copy-start | bytes 8847364
  170.7 2.4 %slice-start = ((bf16[5,8,288,128]{3,2,1,0:T(8,128)(2,1)}), bf16[5,8,192,128]{3,2,1,0:T(8,128)(2,1)S(1)}, s32[]{:S(2)}) async-start(bf16[5,8,288,128]{3,2,1,0:T(8,128)(2,1)} %shard_map.46), calls=%async_computation | async-start | bytes 3932160 | tf_op jit(solution)/shard_map/slice | solution.py:87

commit v2 on v1

--- a/solution.py
+++ b/solution.py
@@ -68,34 +68,11 @@
     return total.astype(BF16)
 
 
-def pack(block, odd):
-    rows, width = block.shape[-2:]
-    half, whole = rows // 2, width - LANES // 2
-    cat = jnp.concatenate
-    e_rest = block[..., whole:]
-    even = cat([block[..., :whole], cat([e_rest[..., :half, :], e_rest[..., half:, :]], -1)], -2)
-    o_rest = block[..., : LANES // 2]
-    odd_ = cat(
-        [block[..., LANES // 2 :], cat([o_rest[..., half:, :], o_rest[..., :half, :]], -1)], -2
-    )
-    return jnp.where(odd, odd_, even)
-
-
-def unpack(packed, rows, odd):
-    cat = jnp.concatenate
-    mid = LANES // 2
-    body, rest = packed[..., :rows, :], packed[..., rows:, :]
-    left, right = rest[..., :mid], rest[..., mid:]
-    even = cat([body, cat([left, right], -2)], -1)
-    odd_ = cat([cat([right, left], -2), body], -1)
-    return jnp.where(odd, odd_, even)
-
-
 def kernel(
     nz, ny, fields,
-    sp, dz_h, dyt_h, out,
-    rin, zst, yst, gz, gy, dz, dyt, g0, visc, vy, fz, fy, dvs, dvr, osend,
-    in_s, in_r, fw_s, fw_r, dv_s, dv_r, g_s, g_r, v_s, v_r, out_s, out_r, w_sem,
+    st_h, vb_h, dz_h, dy_h, out,
+    cells, sp, rout, result, dyv, rin, zst, yst, gz, gy, dz, dyt, g0, visc, vy, fz, fy, dvs, dvr, osend,
+    in_s, in_r, fw_s, fw_r, dv_s, dv_r, g_s, g_r, v_s, v_r, out_s, out_r, w_sem, c_sem, o_sem,
 ):
     me_z, me_y = lax.axis_index("gz"), lax.axis_index("gy")
     yl, zfull = zst.shape[1], zst.shape[2]
@@ -104,6 +81,12 @@
     pw = zfull // pairs
     half = yl // 2
     slots = fields + 1
+    odd = lax.rem(me_z, 2)
+    low = lax.broadcasted_iota(jnp.int32, (half, LANES), 1) < LANES // 2
+    low_all = lax.broadcasted_iota(jnp.int32, (yl, LANES), 1) < LANES // 2
+
+    def turn(x):
+        return pltpu.roll(x, LANES // 2, 1)
 
     def loop(lo, hi, body):
         def step(k, carry):
@@ -129,7 +112,16 @@
         loop(1, n, body)
 
     w1 = pltpu.make_async_copy(dz_h, dz, w_sem.at[0])
-    w2 = pltpu.make_async_copy(dyt_h, dyt, w_sem.at[1])
+    w2 = pltpu.make_async_copy(dy_h, dyv, w_sem.at[1])
+    def fetch(s):
+        if s == 1:
+            return pltpu.make_async_copy(vb_h, cells.at[s], c_sem.at[s])
+        return pltpu.make_async_copy(st_h.at[max(s - 1, 0)], cells.at[s], c_sem.at[s])
+
+    for s in range(slots):
+        fetch(s).start()
+    w2.start()
+    w1.start()
     greet("gz", me_z, nz)
     greet("gy", me_y, ny)
     pl.semaphore_wait(barrier, nz + ny - 2)
@@ -142,9 +134,57 @@
             sp.at[s, other], rin.at[s, slot], in_s.at[s, other], in_r.at[s, slot], "gz", other
         )
 
+    def fold(s, x):
+        t0 = cells[s, x, :, :LANES].astype(F32)
+        rest = cells[s, x, :, LANES:].astype(F32)
+        tt = jnp.concatenate([rest, rest], axis=1)
+
+        @pl.when(odd == 0)
+        def _():
+            sp[s, x, :yl, :] = t0.astype(BF16)
+            sp[s, x, yl:, :] = jnp.where(low, tt[:half], tt[half:]).astype(BF16)
+
+        @pl.when(odd == 1)
+        def _():
+            r0 = turn(t0)
+            sp[s, x, :yl, :] = jnp.where(low_all, r0, tt).astype(BF16)
+            sp[s, x, yl:, :] = jnp.where(low, t0[half:], r0[:half]).astype(BF16)
+
     def start_in(s):
-        loop(1, nz, lambda d: in_copy(s, lax.rem(me_z + d, nz), me_z).start())
+        fetch(s).wait()
+
+        def body(d):
+            other = lax.rem(me_z + d, nz)
+            fold(s, other)
+            in_copy(s, other, me_z).start()
+
+        loop(1, nz, body)
+        fold(s, me_z)
         own_in(s).start()
+
+    def unfold(f, x):
+        body, rest = rout[f, x, :yl, :].astype(F32), rout[f, x, yl:, :].astype(F32)
+        mid = LANES // 2
+
+        @pl.when(odd == 0)
+        def _():
+            result[f, x, :, :LANES] = body.astype(BF16)
+            result[f, x, :half, LANES:] = rest[:, :mid].astype(BF16)
+            result[f, x, half:, LANES:] = turn(rest)[:, :mid].astype(BF16)
+
+        @pl.when(odd == 1)
+        def _():
+            rb = turn(body)
+            result[f, x, :half, :LANES] = jnp.where(low, turn(rest), rb[:half]).astype(BF16)
+            result[f, x, half:, :LANES] = jnp.where(low, rest, rb[half:]).astype(BF16)
+            result[f, x, :, LANES:] = rb[:, :mid].astype(BF16)
+
+    def transpose_dy():
+        def body(k):
+            c = pl.multiple_of(k * LANES, LANES)
+            dyt[pl.ds(c, LANES), :] = jnp.transpose(dyv[:, pl.ds(c, LANES)])
+
+        loop(0, dyv.shape[0] // LANES, body)
 
     def wait_in(s):
         loop(1, nz, lambda d: in_copy(s, lax.rem(me_z + d, nz), lax.rem(me_z + d, nz)).wait_recv())
@@ -201,20 +241,15 @@
 
     def out_copy(f, other, slot):
         return remote(
-            osend.at[f, other], out.at[f, slot], out_s.at[f, other], out_r.at[f, slot],
+            osend.at[f, other], rout.at[f, slot], out_s.at[f, other], out_r.at[f, slot],
             "gz", other,
         )
 
     def own_out(f):
-        return pltpu.make_async_copy(osend.at[f, me_z], out.at[f, me_z], out_r.at[f, me_z])
+        return pltpu.make_async_copy(osend.at[f, me_z], rout.at[f, me_z], out_r.at[f, me_z])
 
     def pair_cols(m):
         return pl.multiple_of(m * pw, LANES)
-
-    low = lax.broadcasted_iota(jnp.int32, (half, LANES), 1) < LANES // 2
-
-    def turn(x):
-        return pltpu.roll(x, LANES // 2, 1)
 
     def gather_lines(s):
         wait_in(s)
@@ -311,11 +346,11 @@
         loop(1, nz, lambda d: out_copy(f, lax.rem(me_z + d, nz), me_z).start())
         own_out(f).start()
 
-    loop(0, slots, start_in)
-    w1.start()
-    w2.start()
+    for s in range(slots):
+        start_in(s)
+    w2.wait()
+    transpose_dy()
     w1.wait()
-    w2.wait()
     stage_a(0, 0)
     stage_b(0, 0)
     dens_y.start()
@@ -356,12 +391,19 @@
         def body(d):
             other = lax.rem(me_z + d, nz)
             out_copy(f, other, other).wait_recv()
+            unfold(f, other)
             out_copy(f, other, me_z).wait_send()
 
+        own_out(f).wait()
+        unfold(f, me_z)
         loop(1, nz, body)
-        own_out(f).wait()
+        store(f).start()
+
+    def store(f):
+        return pltpu.make_async_copy(result.at[f], out.at[f], o_sem.at[f])
 
     loop(0, fields, finish)
+    loop(0, fields, lambda f: store(f).wait())
 
 
 def by_planes(nz, ny, state, visc_base, dz_op, dy_op):
@@ -370,17 +412,20 @@
     zw = zfull // ny
     slots = fields + 1
     prow = yl + yl // 2
-    odd = lax.rem(lax.axis_index("gz"), 2) == 1
-    sp = pack(jnp.concatenate([state[:1], visc_base[None], state[1:]], 0), odd)
     any_ = pl.BlockSpec(memory_space=pl.ANY)
     vm = lambda *shape: pltpu.VMEM(shape, BF16)
     dma = lambda *shape: pltpu.SemaphoreType.DMA(shape)
-    packed = pl.pallas_call(
+    return pl.pallas_call(
         functools.partial(kernel, nz, ny, fields),
-        out_shape=jax.ShapeDtypeStruct((fields, planes, prow, LANES), BF16),
-        in_specs=[any_] * 3,
+        out_shape=jax.ShapeDtypeStruct(state.shape, BF16),
+        in_specs=[any_] * 4,
         out_specs=any_,
         scratch_shapes=[
+            vm(slots, planes, yl, zl),
+            vm(slots, nz, prow, LANES),
+            vm(fields, nz, prow, LANES),
+            vm(fields, planes, yl, zl),
+            vm(yfull, yfull),
             vm(slots, nz, prow, LANES),
             vm(slots, yl, zfull),
             vm(fields, yfull, zw),
@@ -401,13 +446,12 @@
             dma(fields, ny), dma(fields, ny),
             dma(ny), dma(ny), dma(ny), dma(ny),
             dma(fields, nz), dma(fields, nz),
-            dma(2),
+            dma(2), dma(slots), dma(fields),
         ],
         compiler_params=pltpu.CompilerParams(
             collective_id=0, has_side_effects=True, vmem_limit_bytes=56 * 2**20
         ),
-    )(sp, dz_op, dy_op.T)
-    return unpack(packed, yl, odd)
+    )(state, visc_base, dz_op, dy_op)
 
 
 def on_device(nz, ny, state, visc_base, dz_op, dy_op):

time: 177 us -> 160 us (0.904)
  other arithmetic: 10.4 us -> 0 us
  local copies, waits for them, and re-layouts: 12.4 us -> 4.48 us
    select_n x2 -> x0, other arithmetic: 9.53 us -> none  [the longest x1 5.86 us: pack(): return jnp.where(odd, odd_, even)]
    slice x9 -> x0, local copies, waits for them, and re-layouts: 8 us -> none  [the longest x1 2.72 us: pack(): block[..., :whole]]
    unnamed x5 -> x1, local copies, waits for them, and re-layouts: 4.43 us -> 4.48 us
where the time goes in v2:
time: 160 us
  Pallas kernels  155 us (97%)
  local copies, waits for them, and re-layouts  4.48 us (3%)
    pallas_call x1, Pallas kernels, by_planes(): pl.pallas_call(functools.partial(kernel, nz, ny, fields), out_shape=jax.S...  155 us
    unnamed x1, local copies, waits for them, and re-layouts  4.48 us

profile of v2, /device:TPU:29, one launch (start us, length us, event | category | flops | bytes accessed | tf_op | source)
XLA Modules:
  0.0 159.7 jit_solution(5686611577528132851)
XLA Ops:
  0.0 155.2 %shard_map.46 = bf16[5,8,192,192]{3,2,1,0:T(8,128)(2,1)} custom-call(bf16[5,8,192,192]{3,2,1,0:T(8,128)(2,1)} %st_h.1, bf16[8,192,192]{2,1,0:T(8,128)(2,1)} %vb_h.1, bf16[1536,1536]{1,0:T(8,128)(2,1)} %dz_h.1, bf16[768,768]{1,0:T(8,128)(2,1)} %dy_h.1), custom_call_target="tpu_custom_call" | custom-call | tf_op jit(solution)/shard_map/pallas_call | solution.py:418
  155.2 4.5 %copy.6 = bf16[5,8,192,192]{3,2,1,0:T(8,128)(2,1)} copy(bf16[5,8,192,192]{3,2,1,0:T(8,128)(2,1)} %shard_map.46) | data formatting | bytes 5898240

commit v3 on v2

--- a/solution.py
+++ b/solution.py
@@ -71,8 +71,8 @@
 def kernel(
     nz, ny, fields,
     st_h, vb_h, dz_h, dy_h, out,
-    cells, sp, rout, result, dyv, rin, zst, yst, gz, gy, dz, dyt, g0, visc, vy, fz, fy, dvs, dvr, osend,
-    in_s, in_r, fw_s, fw_r, dv_s, dv_r, g_s, g_r, v_s, v_r, out_s, out_r, w_sem, c_sem, o_sem,
+    cells, sp, rout, dyv, rin, zst, yst, gz, gy, dz, dyt, g0, visc, vy, fz, fy, dvs, dvr, osend,
+    in_s, in_r, fw_s, fw_r, dv_s, dv_r, g_s, g_r, v_s, v_r, out_s, out_r, w_sem, c_sem,
 ):
     me_z, me_y = lax.axis_index("gz"), lax.axis_index("gy")
     yl, zfull = zst.shape[1], zst.shape[2]
@@ -113,18 +113,20 @@
 
     w1 = pltpu.make_async_copy(dz_h, dz, w_sem.at[0])
     w2 = pltpu.make_async_copy(dy_h, dyv, w_sem.at[1])
+
     def fetch(s):
         if s == 1:
             return pltpu.make_async_copy(vb_h, cells.at[s], c_sem.at[s])
         return pltpu.make_async_copy(st_h.at[max(s - 1, 0)], cells.at[s], c_sem.at[s])
 
-    for s in range(slots):
+    fetch(0).start()
+    greet("gz", me_z, nz)
+    greet("gy", me_y, ny)
+    fetch(0).wait()
+    for s in range(1, slots):
         fetch(s).start()
     w2.start()
     w1.start()
-    greet("gz", me_z, nz)
-    greet("gy", me_y, ny)
-    pl.semaphore_wait(barrier, nz + ny - 2)
 
     def own_in(s):
         return pltpu.make_async_copy(sp.at[s, me_z], rin.at[s, me_z], in_r.at[s, me_z])
@@ -151,15 +153,21 @@
             sp[s, x, yl:, :] = jnp.where(low, t0[half:], r0[:half]).astype(BF16)
 
     def start_in(s):
-        fetch(s).wait()
+        if s > 0:
+            fetch(s).wait()
 
         def body(d):
             other = lax.rem(me_z + d, nz)
-            fold(s, other)
+            if s > 0:
+                fold(s, other)
             in_copy(s, other, me_z).start()
 
+        if s == 0:
+            loop(0, nz, lambda x: fold(s, x))
+            pl.semaphore_wait(barrier, nz + ny - 2)
         loop(1, nz, body)
-        fold(s, me_z)
+        if s > 0:
+            fold(s, me_z)
         own_in(s).start()
 
     def unfold(f, x):
@@ -168,16 +176,16 @@
 
         @pl.when(odd == 0)
         def _():
-            result[f, x, :, :LANES] = body.astype(BF16)
-            result[f, x, :half, LANES:] = rest[:, :mid].astype(BF16)
-            result[f, x, half:, LANES:] = turn(rest)[:, :mid].astype(BF16)
+            out[f, x, :, :LANES] = body.astype(BF16)
+            out[f, x, :half, LANES:] = rest[:, :mid].astype(BF16)
+            out[f, x, half:, LANES:] = turn(rest)[:, :mid].astype(BF16)
 
         @pl.when(odd == 1)
         def _():
             rb = turn(body)
-            result[f, x, :half, :LANES] = jnp.where(low, turn(rest), rb[:half]).astype(BF16)
-            result[f, x, half:, :LANES] = jnp.where(low, rest, rb[half:]).astype(BF16)
-            result[f, x, :, LANES:] = rb[:, :mid].astype(BF16)
+            out[f, x, :half, :LANES] = jnp.where(low, turn(rest), rb[:half]).astype(BF16)
+            out[f, x, half:, :LANES] = jnp.where(low, rest, rb[half:]).astype(BF16)
+            out[f, x, :, LANES:] = rb[:, :mid].astype(BF16)
 
     def transpose_dy():
         def body(k):
@@ -389,21 +397,16 @@
         divs(f).sent()
 
         def body(d):
-            other = lax.rem(me_z + d, nz)
+            other = lax.rem(me_z + nz - d, nz)
             out_copy(f, other, other).wait_recv()
             unfold(f, other)
-            out_copy(f, other, me_z).wait_send()
 
         own_out(f).wait()
         unfold(f, me_z)
         loop(1, nz, body)
-        store(f).start()
-
-    def store(f):
-        return pltpu.make_async_copy(result.at[f], out.at[f], o_sem.at[f])
+        loop(1, nz, lambda d: out_copy(f, lax.rem(me_z + d, nz), me_z).wait_send())
 
     loop(0, fields, finish)
-    loop(0, fields, lambda f: store(f).wait())
 
 
 def by_planes(nz, ny, state, visc_base, dz_op, dy_op):
@@ -412,19 +415,19 @@
     zw = zfull // ny
     slots = fields + 1
     prow = yl + yl // 2
-    any_ = pl.BlockSpec(memory_space=pl.ANY)
+    keep = functools.partial(pltpu.with_memory_space_constraint, memory_space=pltpu.HBM)
+    hbm = pl.BlockSpec(memory_space=pltpu.HBM)
     vm = lambda *shape: pltpu.VMEM(shape, BF16)
     dma = lambda *shape: pltpu.SemaphoreType.DMA(shape)
     return pl.pallas_call(
         functools.partial(kernel, nz, ny, fields),
         out_shape=jax.ShapeDtypeStruct(state.shape, BF16),
-        in_specs=[any_] * 4,
-        out_specs=any_,
+        in_specs=[hbm] * 4,
+        out_specs=pl.BlockSpec(memory_space=pltpu.VMEM),
         scratch_shapes=[
             vm(slots, planes, yl, zl),
             vm(slots, nz, prow, LANES),
             vm(fields, nz, prow, LANES),
-            vm(fields, planes, yl, zl),
             vm(yfull, yfull),
             vm(slots, nz, prow, LANES),
             vm(slots, yl, zfull),
@@ -446,12 +449,12 @@
             dma(fields, ny), dma(fields, ny),
             dma(ny), dma(ny), dma(ny), dma(ny),
             dma(fields, nz), dma(fields, nz),
-            dma(2), dma(slots), dma(fields),
+            dma(2), dma(slots),
         ],
         compiler_params=pltpu.CompilerParams(
-            collective_id=0, has_side_effects=True, vmem_limit_bytes=56 * 2**20
+            collective_id=0, has_side_effects=True, vmem_limit_bytes=46 * 2**20
         ),
-    )(state, visc_base, dz_op, dy_op)
+    )(keep(state), keep(visc_base), keep(dz_op), keep(dy_op))
 
 
 def on_device(nz, ny, state, visc_base, dz_op, dy_op):

time: 160 us -> 155 us (0.969)
  local copies, waits for them, and re-layouts: 4.48 us -> 1.93 us
  Pallas kernels: 155 us -> 153 us
    unnamed x1, local copies, waits for them, and re-layouts: 4.48 us -> 1.93 us
    pallas_call x1, Pallas kernels: 155 us -> 153 us  [by_planes(): pl.pallas_call(functools.partial(kernel, nz, ny, fields), out_shape=jax.S...]
where the time goes in v3:
time: 155 us
  Pallas kernels  153 us (99%)
  local copies, waits for them, and re-layouts  1.93 us (1%)
    pallas_call x1, Pallas kernels, by_planes(): pl.pallas_call(functools.partial(kernel, nz, ny, fields), out_shape=jax.S...  153 us

profile of v3, /device:TPU:29, one launch (start us, length us, event | category | flops | bytes accessed | tf_op | source)
XLA Modules:
  0.0 155.1 jit_solution(10373708277934796677)
XLA Ops:
  0.0 153.1 %shard_map.46 = bf16[5,8,192,192]{3,2,1,0:T(8,128)(2,1)S(1)} custom-call(bf16[5,8,192,192]{3,2,1,0:T(8,128)(2,1)} %st_h.1, bf16[8,192,192]{2,1,0:T(8,128)(2,1)} %vb_h.1, bf16[1536,1536]{1,0:T(8,128)(2,1)} %dz_h.1, bf16[768,768]{1,0:T(8,128)(2,1)} %dy_h.1), custom_call_target="tpu_custom_call" | custom-call | tf_op jit(solution)/shard_map/pallas_call | solution.py:422
  153.1 1.9 %copy.6 = bf16[5,8,192,192]{3,2,1,0:T(8,128)(2,1)} copy(bf16[5,8,192,192]{3,2,1,0:T(8,128)(2,1)S(1)} %shard_map.46) | data formatting | bytes 5898240
